TPU v7x, 32 devices: a whole 2x2x4 slice. The times are simulated.
32 devices in a mesh: tmpl: 4 (over y, x), tm: 4 (over z), rec: 2 (over core).
Axes of the slice: x: 2, y: 2, z: 4, core: 2. Of those that a mesh axis runs over, the one named last changes fastest.
Arguments:
- corpus: bfloat16 [8, 8192, 128], P(('tmpl', 'rec'), 'tm'), may hold values from -16 to 16
- templates: bfloat16 [512, 64, 128], P(('tmpl', 'rec')), may hold values from -4 to 4
- rec_ids: int32 [8, 8192], P(('tmpl', 'rec'), 'tm'), may hold values from 0 to 15, never falling along the last dimension, each value on 1 to 1024 neighbouring positions
- valid_frames: int32 [8, 4], P(('tmpl', 'rec'), 'tm'), may hold values from 1024 to 2048
Outputs:
- rec_scores: float32 [8, 16, 512], P(('tmpl', 'rec'))
- template_scores: float32 [512], replicated
Inputs may be any that keep to these rules, and one draw needn't show every extreme that they name: `rec_ids`: recording numbers never fall along a group's chain; each recording holds 1 to 1024 frames.
All inputs are finite; a program needn't handle non-finite values.
Results may differ from a plain program's by a relative error of at most 0.0003.
Values may be sent and summed in bfloat16 or wider, within the bound.
A program may use at most 64 MiB of HBM per device.

v0:
```python
import jax
import jax.numpy as jnp
from jax import lax
from jax.sharding import PartitionSpec as P

RECS = 16


def shifted(x, axis, by):
    size = lax.axis_size(axis)
    pairs = [(i, i + by) for i in range(size) if 0 <= i + by < size]
    return lax.ppermute(x, axis, pairs)


def merged(part, axis, combine):
    gathered = jax.tree.map(lambda a: lax.all_gather(a, axis), part)

    def take(source):
        return jax.tree.map(lambda a: lax.dynamic_index_in_dim(a, source, 0, False), gathered)

    return lax.fori_loop(
        1, lax.axis_size(axis), lambda source, state: combine(state, take(source)), take(0)
    )


def slab_stats(scores, frame_ids, usable_count):
    length = scores.shape[-1]
    margin = frame_ids.shape[0] - length
    positions = jnp.arange(length, dtype=jnp.int32)
    usable = (positions < usable_count) & (frame_ids[margin:] == frame_ids[:length])
    labels = jnp.arange(RECS, dtype=jnp.int32)
    member = ((frame_ids[:length][None, :] == labels[:, None]) & usable[None, :]).astype(
        jnp.float32
    )

    def top_of(label_row):
        return jnp.max(jnp.where(label_row[None, :] > 0, scores, -jnp.inf), axis=1)

    peaks = jnp.maximum(lax.map(top_of, member), 0.0)
    spread = jnp.dot(peaks.T, member, precision=lax.Precision.HIGHEST)
    weights = jnp.where(usable[None, :], jnp.exp(scores - spread), 0.0)
    totals = jnp.dot(member, weights.T, precision=lax.Precision.HIGHEST)
    return (peaks, totals)


def correlate(extended, bank, score_scale):
    result = lax.conv_general_dilated(
        extended,
        bank,
        (1,),
        "VALID",
        dimension_numbers=("NWC", "OWI", "NCW"),
        preferred_element_type=jnp.float32,
    )
    return result * score_scale


def merge_pair(left_side, right_side):
    highest = jnp.maximum(left_side[0], right_side[0])
    summed = left_side[1] * jnp.exp(left_side[0] - highest) + right_side[1] * jnp.exp(
        right_side[0] - highest
    )
    return (highest, summed)


def collapse(peaks, totals):
    highest = jnp.max(peaks, axis=0)
    summed = jnp.sum(totals * jnp.exp(peaks - highest[None, :]), axis=0)
    return (highest, summed)


def on_device(corpus, templates, rec_ids, valid_frames):
    bank_rows, frames, bins = templates.shape
    margin = frames - 1
    score_scale = (frames * bins) ** (-0.5)
    rim_data, rim_ids = shifted((corpus[:, :margin], rec_ids[:, :margin] + 1), "tm", -1)
    extended = jnp.concatenate([corpus, rim_data], axis=1)
    frame_ids = jnp.concatenate([rec_ids, rim_ids - 1], axis=1)
    groups = lax.axis_size(("tmpl", "rec"))
    all_rows = bank_rows * groups
    initial = jnp.zeros((RECS, all_rows), jnp.float32)
    offset = jnp.int32(0)
    scores = correlate(
        extended, lax.all_gather(templates, ("tmpl", "rec"), axis=0, tiled=True), score_scale
    )[0]
    peaks, totals = slab_stats(scores, frame_ids[0], valid_frames[0, 0])
    anchor = jnp.zeros((), offset.dtype)
    peaks, totals = (
        lax.dynamic_update_slice(initial, peaks, (anchor, offset)),
        lax.dynamic_update_slice(initial, totals, (anchor, offset)),
    )
    chain_peaks, chain_totals = merged((peaks, totals), "tm", merge_pair)
    rec_scores = chain_peaks + jnp.log(jnp.exp(-chain_peaks) + chain_totals)
    highest, summed = collapse(chain_peaks, chain_totals)
    highest, summed = merged((highest, summed), ("tmpl", "rec"), merge_pair)
    template_scores = highest + jnp.log(jnp.exp(-highest) + summed)
    return (rec_scores[None], template_scores)


def solution(mesh):
    return jax.shard_map(
        on_device,
        mesh=mesh,
        in_specs=(
            P(("tmpl", "rec"), "tm", None),
            P(("tmpl", "rec"), None, None),
            P(("tmpl", "rec"), "tm"),
            P(("tmpl", "rec"), "tm"),
        ),
        out_specs=(P(("tmpl", "rec"), None, None), P()),
        check_vma=False,
    )
```

profile of v0, /device:TPU:0, one launch (start us, length us, event | category | flops | bytes accessed | tf_op | source)
XLA Modules:
  0.0 205.2 jit_solution(6083373414790854648)
XLA Ops:
  7.2 3.0 %copy.14 = bf16[64,64,128]{2,0,1:T(8,128)(2,1)} copy(bf16[64,64,128]{2,1,0:T(8,128)(2,1)} %param.11) | data formatting | bytes 2097152 | tf_op args[1]
  10.9 1.3 collective-permute-start
  12.9 1.3 collective-permute-start.1
  14.8 2.5 %collective-permute-done = s32[1,63]{1,0:T(1,128)S(1)} collective-permute-done((s32[1,63]{1,0:T(1,128)S(1)}, s32[1,63]{1,0:T(1,128)S(1)}, u32[]{:S(2)}, u32[]{:S(2)}) %collective-permute-start) | collective-permute-done | bytes 284 | tf_op jit(solution)/shard_map/ppermute | solution.py:12
  21.4 46.0 %all-gather.8.cloned.1.call-done = bf16[512,64,128]{2,0,1:T(8,128)(2,1)} async-done(((bf16[64,64,128]{2,0,1:T(8,128)(2,1)}), bf16[512,64,128]{2,0,1:T(8,128)(2,1)}) %all-gather.8.cloned.1.call-update) | async-done | bytes 8388624 | tf_op jit(solution)/shard_map/all_gather | solution.py:84
  67.5 27.7 %select_multiply_fusion = f32[8,264,512]{2,0,1:T(8,128)S(1)} fusion(pred[8,264]{0,1:T(8,128)(4,1)S(1)} %copy-done.2, bf16[512,64,128]{2,0,1:T(8,128)(2,1)} %all-gather.8.cloned.1.call-done, bf16[1,7,63,128]{3,1,2,0:T(8,128)(2,1)S(1)} %slice.28, bf16[1,8,264,128]{3,1,2,0:T(8,128)(2,1)S(1)} %copy.13), kind=kOutput, calls=%fused_computation.10 | convolution fusion | flops 17720911872 | bytes 13369664 | tf_op jit(solution)/shard_map/conv_general_dilated | solution.py:47
  95.2 2.5 %copy.15 = f32[8,264,512]{2,1,0:T(8,128)S(1)} copy(f32[8,264,512]{2,0,1:T(8,128)S(1)} %select_multiply_fusion) | data formatting | bytes 8650752 | tf_op jit(solution)/shard_map/mul | solution.py:55
  97.7 2.4 %slice.29 = f32[1,2048,512]{2,1,0:T(8,128)} slice(f32[1,2112,512]{2,1,0:T(8,128)S(1)} %bitcast.59), slice={[0:1], [0:2048], [0:512]} | slice | bytes 8388608 | tf_op jit(solution)/shard_map/mul | solution.py:55
  100.1 5.4 %copy.19 = f32[1,2048,512]{1,2,0:T(8,128)} copy(f32[1,2048,512]{2,1,0:T(8,128)} %slice.29) | data formatting | bytes 8388608
  105.5 42.7 %while.47 = (s32[]{:T(128)}, f32[16,512]{1,0:T(8,128)S(1)}, f32[16,2048]{1,0:T(8,128)S(1)}, f32[512,2048]{1,0:T(8,128)}) while((s32[]{:T(128)}, f32[16,512]{1,0:T(8,128)S(1)}, f32[16,2048]{1,0:T(8,128)S(1)}, f32[512,2048]{1,0:T(8,128)}) %tuple.118), condition=%wide.region_2.3_spmd.clone, body=%wide.region_0.2_spmd.sunk.clone | while | flops 2098690 | bytes 4212797 | solution.py:39
  105.6 2.5 %select_reduce_fusion.3 = f32[512]{0:T(512)S(1)} fusion(f32[512,2048]{1,0:T(8,128)} %get-tuple-element.490, pred[2048]{0:T(1024)(128)(4,1)S(1)} %compare_reduce_fusion.3), kind=kLoop, calls=%fused_computation.8.clone.1.clone | loop fusion | flops 2096640 | bytes 4198400 | tf_op jit(solution)/shard_map/while/body/eval_jaxpr/reduce_max | solution.py:37
  108.2 2.5 %select_reduce_fusion.3 = f32[512]{0:T(512)S(1)} fusion(f32[512,2048]{1,0:T(8,128)} %get-tuple-element.490, pred[2048]{0:T(1024)(128)(4,1)S(1)} %compare_reduce_fusion.3), kind=kLoop, calls=%fused_computation.8.clone.1.clone | loop fusion | flops 2096640 | bytes 4198400 | tf_op jit(solution)/shard_map/while/body/eval_jaxpr/reduce_max | solution.py:37
  110.9 2.5 %select_reduce_fusion.3 = f32[512]{0:T(512)S(1)} fusion(f32[512,2048]{1,0:T(8,128)} %get-tuple-element.490, pred[2048]{0:T(1024)(128)(4,1)S(1)} %compare_reduce_fusion.3), kind=kLoop, calls=%fused_computation.8.clone.1.clone | loop fusion | flops 2096640 | bytes 4198400 | tf_op jit(solution)/shard_map/while/body/eval_jaxpr/reduce_max | solution.py:37
  113.6 2.5 %select_reduce_fusion.3 = f32[512]{0:T(512)S(1)} fusion(f32[512,2048]{1,0:T(8,128)} %get-tuple-element.490, pred[2048]{0:T(1024)(128)(4,1)S(1)} %compare_reduce_fusion.3), kind=kLoop, calls=%fused_computation.8.clone.1.clone | loop fusion | flops 2096640 | bytes 4198400 | tf_op jit(solution)/shard_map/while/body/eval_jaxpr/reduce_max | solution.py:37
  116.2 2.5 %select_reduce_fusion.3 = f32[512]{0:T(512)S(1)} fusion(f32[512,2048]{1,0:T(8,128)} %get-tuple-element.490, pred[2048]{0:T(1024)(128)(4,1)S(1)} %compare_reduce_fusion.3), kind=kLoop, calls=%fused_computation.8.clone.1.clone | loop fusion | flops 2096640 | bytes 4198400 | tf_op jit(solution)/shard_map/while/body/eval_jaxpr/reduce_max | solution.py:37
  118.9 2.5 %select_reduce_fusion.3 = f32[512]{0:T(512)S(1)} fusion(f32[512,2048]{1,0:T(8,128)} %get-tuple-element.490, pred[2048]{0:T(1024)(128)(4,1)S(1)} %compare_reduce_fusion.3), kind=kLoop, calls=%fused_computation.8.clone.1.clone | loop fusion | flops 2096640 | bytes 4198400 | tf_op jit(solution)/shard_map/while/body/eval_jaxpr/reduce_max | solution.py:37
  121.6 2.5 %select_reduce_fusion.3 = f32[512]{0:T(512)S(1)} fusion(f32[512,2048]{1,0:T(8,128)} %get-tuple-element.490, pred[2048]{0:T(1024)(128)(4,1)S(1)} %compare_reduce_fusion.3), kind=kLoop, calls=%fused_computation.8.clone.1.clone | loop fusion | flops 2096640 | bytes 4198400 | tf_op jit(solution)/shard_map/while/body/eval_jaxpr/reduce_max | solution.py:37
  124.3 2.5 %select_reduce_fusion.3 = f32[512]{0:T(512)S(1)} fusion(f32[512,2048]{1,0:T(8,128)} %get-tuple-element.490, pred[2048]{0:T(1024)(128)(4,1)S(1)} %compare_reduce_fusion.3), kind=kLoop, calls=%fused_computation.8.clone.1.clone | loop fusion | flops 2096640 | bytes 4198400 | tf_op jit(solution)/shard_map/while/body/eval_jaxpr/reduce_max | solution.py:37
  126.9 2.5 %select_reduce_fusion.3 = f32[512]{0:T(512)S(1)} fusion(f32[512,2048]{1,0:T(8,128)} %get-tuple-element.490, pred[2048]{0:T(1024)(128)(4,1)S(1)} %compare_reduce_fusion.3), kind=kLoop, calls=%fused_computation.8.clone.1.clone | loop fusion | flops 2096640 | bytes 4198400 | tf_op jit(solution)/shard_map/while/body/eval_jaxpr/reduce_max | solution.py:37
  129.6 2.5 %select_reduce_fusion.3 = f32[512]{0:T(512)S(1)} fusion(f32[512,2048]{1,0:T(8,128)} %get-tuple-element.490, pred[2048]{0:T(1024)(128)(4,1)S(1)} %compare_reduce_fusion.3), kind=kLoop, calls=%fused_computation.8.clone.1.clone | loop fusion | flops 2096640 | bytes 4198400 | tf_op jit(solution)/shard_map/while/body/eval_jaxpr/reduce_max | solution.py:37
  132.3 2.5 %select_reduce_fusion.3 = f32[512]{0:T(512)S(1)} fusion(f32[512,2048]{1,0:T(8,128)} %get-tuple-element.490, pred[2048]{0:T(1024)(128)(4,1)S(1)} %compare_reduce_fusion.3), kind=kLoop, calls=%fused_computation.8.clone.1.clone | loop fusion | flops 2096640 | bytes 4198400 | tf_op jit(solution)/shard_map/while/body/eval_jaxpr/reduce_max | solution.py:37
  134.9 2.5 %select_reduce_fusion.3 = f32[512]{0:T(512)S(1)} fusion(f32[512,2048]{1,0:T(8,128)} %get-tuple-element.490, pred[2048]{0:T(1024)(128)(4,1)S(1)} %compare_reduce_fusion.3), kind=kLoop, calls=%fused_computation.8.clone.1.clone | loop fusion | flops 2096640 | bytes 4198400 | tf_op jit(solution)/shard_map/while/body/eval_jaxpr/reduce_max | solution.py:37
  137.6 2.5 %select_reduce_fusion.3 = f32[512]{0:T(512)S(1)} fusion(f32[512,2048]{1,0:T(8,128)} %get-tuple-element.490, pred[2048]{0:T(1024)(128)(4,1)S(1)} %compare_reduce_fusion.3), kind=kLoop, calls=%fused_computation.8.clone.1.clone | loop fusion | flops 2096640 | bytes 4198400 | tf_op jit(solution)/shard_map/while/body/eval_jaxpr/reduce_max | solution.py:37
  140.3 2.5 %select_reduce_fusion.3 = f32[512]{0:T(512)S(1)} fusion(f32[512,2048]{1,0:T(8,128)} %get-tuple-element.490, pred[2048]{0:T(1024)(128)(4,1)S(1)} %compare_reduce_fusion.3), kind=kLoop, calls=%fused_computation.8.clone.1.clone | loop fusion | flops 2096640 | bytes 4198400 | tf_op jit(solution)/shard_map/while/body/eval_jaxpr/reduce_max | solution.py:37
  142.9 2.5 %select_reduce_fusion.3 = f32[512]{0:T(512)S(1)} fusion(f32[512,2048]{1,0:T(8,128)} %get-tuple-element.490, pred[2048]{0:T(1024)(128)(4,1)S(1)} %compare_reduce_fusion.3), kind=kLoop, calls=%fused_computation.8.clone.1.clone | loop fusion | flops 2096640 | bytes 4198400 | tf_op jit(solution)/shard_map/while/body/eval_jaxpr/reduce_max | solution.py:37
  145.6 2.5 %select_reduce_fusion.3 = f32[512]{0:T(512)S(1)} fusion(f32[512,2048]{1,0:T(8,128)} %get-tuple-element.490, pred[2048]{0:T(1024)(128)(4,1)S(1)} %compare_reduce_fusion.3), kind=kLoop, calls=%fused_computation.8.clone.1.clone | loop fusion | flops 2096640 | bytes 4198400 | tf_op jit(solution)/shard_map/while/body/eval_jaxpr/reduce_max | solution.py:37
  148.2 1.9 fusion.21
  150.4 2.5 %fusion.2 = f32[16,512]{1,0:T(8,128)S(1)} fusion(f32[512,2048]{1,0:T(8,128)S(1)} %fusion.21, pred[2048]{0:T(1024)(128)(4,1)S(1)} %and_reduce_fusion, s32[2048]{0:T(1024)S(1)} %bitcast.68, f32[1,2048,512]{1,2,0:T(8,128)S(1)} %bitcast.58), kind=kOutput, calls=%fused_computation.11 | convolution fusion | flops 203489280 | bytes 8431616 | tf_op jit(solution)/shard_map/dot_general | solution.py:42
  152.9 13.4 %all-gather.1 = f32[64,512]{1,0:T(8,128)S(1)} all-gather(f32[16,512]{1,0:T(8,128)S(1)} %fusion.2), channel_id=3, replica_groups=mesh['tmpl'=4,'tm'=4,'rec'=2] {'tm'}, dimensions={0}, use_global_device_ids=true | all-gather | bytes 163840 | tf_op jit(solution)/shard_map/all_gather | solution.py:16
  166.4 13.4 %all-gather = f32[64,512]{1,0:T(8,128)S(1)} all-gather(f32[16,512]{1,0:T(8,128)S(1)} %broadcast_maximum_fusion), channel_id=2, replica_groups=mesh['tmpl'=4,'tm'=4,'rec'=2] {'tm'}, dimensions={0}, use_global_device_ids=true | all-gather | bytes 163840 | tf_op jit(solution)/shard_map/all_gather | solution.py:16
  180.6 8.8 %all-gather.5 = f32[8,1,512]{2,1,0:T(1,128)S(1)} all-gather(f32[1,1,512]{2,1,0:T(1,128)S(1)} %bitcast.74), channel_id=5, replica_groups=mesh['tmpl'=4,'tm'=4,'rec'=2] {'tmpl','rec'}, dimensions={0}, use_global_device_ids=true | all-gather | bytes 18432 | tf_op jit(solution)/shard_map/all_gather | solution.py:16
  189.4 7.9 %all-gather.4 = f32[8,1,512]{2,1,0:T(1,128)S(1)} all-gather(f32[1,1,512]{2,1,0:T(1,128)S(1)} %bitcast.73), channel_id=4, replica_groups=mesh['tmpl'=4,'tm'=4,'rec'=2] {'tmpl','rec'}, dimensions={0}, use_global_device_ids=true | all-gather | bytes 18432 | tf_op jit(solution)/shard_map/all_gather | solution.py:16
  (79 shorter events, 9.6 us)
Async XLA Ops:
  7.2 60.3 %copy-start.2 = (pred[8,264]{0,1:T(8,128)(4,1)S(1)}, pred[8,264]{0,1:T(8,128)(4,1)}, u32[]{:S(2)}) copy-start(pred[8,264]{0,1:T(8,128)(4,1)} %constant.121) | copy-start | bytes 6340
  7.2 60.3 %all-gather.8.cloned.1.call-start = ((), (), s32[]{:S(2)}) async-start(), calls=%async_computation | async-start | bytes 9437184 | tf_op jit(solution)/shard_map/all_gather | solution.py:84
  10.9 6.4 %collective-permute-start = (s32[1,63]{1,0:T(1,128)S(1)}, s32[1,63]{1,0:T(1,128)S(1)}, u32[]{:S(2)}, u32[]{:S(2)}) collective-permute-start(s32[1,63]{1,0:T(1,128)S(1)} %slice_add_fusion), channel_id=1, source_target_pairs={{2,0},{4,2},{6,4},{3,1},{5,3},{7,5},{10,8},{12,10},{14,12},{11,9},... | collective-permute-start | bytes 764 | tf_op jit(solution)/shard_map/ppermute | solution.py:12
  12.9 7.3 %collective-permute-start.1 = (bf16[1,63,128]{2,1,0:T(8,128)(2,1)S(1)}, bf16[1,63,128]{2,1,0:T(8,128)(2,1)S(1)}, u32[]{:S(2)}, u32[]{:S(2)}) collective-permute-start(bf16[1,63,128]{2,1,0:T(8,128)(2,1)S(1)} %slice.19), channel_id=1, source_target_pairs={{2,0},{4,2},{6,4},{3,1},{5,3},{7,5},{10,8},{12,10},{14,12},{11,9},... | collective-permute-start | bytes 48392 | tf_op jit(solution)/shard_map/ppermute | solution.py:12
  105.5 42.7 %copy-start.1 = (s32[1,2048]{1,0:T(1,128)S(1)}, s32[1,2048]{1,0:T(1,128)}, u32[]{:S(2)}) copy-start(s32[1,2048]{1,0:T(1,128)} %param.12) | copy-start | bytes 24580
  148.2 2.2 %copy-start = (f32[512,2048]{1,0:T(8,128)S(1)}, f32[512,2048]{1,0:T(8,128)}, u32[]{:S(2)}) copy-start(f32[512,2048]{1,0:T(8,128)} %get-tuple-element.522) | copy-start | bytes 12582916
Sparse Core Ops, SparseCore 0:
  10.3 57.0 all-gather.7
where the time goes:
time: 206 us; the launch traced here: 205 us
  waiting for transfers between devices  49.8 us (24%)
  other arithmetic  46.3 us (22%)
  blocking collectives  43.6 us (21%)
  matrix products  32.1 us (16%)
  local copies, waits for them, and re-layouts  15.4 us (7%)
  between operations  14.8 us (7%)
  starting transfers between devices  2.6 us (1%)
    all_gather x1, waiting for transfers between devices, on_device(): lax.all_gather(templates, ('tmpl', 'rec'), axis=0, tiled=True)  46 us
    all_gather x4, blocking collectives, merged(): gathered = jax.tree.map(lambda a: lax.all_gather(a, axis), part)  43.6 us
    reduce_max x16, other arithmetic, top_of(): return jnp.max(jnp.where(label_row[None, :] > 0, scores, -jnp.inf), axis=1)  40.7 us
    conv_general_dilated x1, matrix products, correlate(): lax.conv_general_dilated(extended, bank, (1,), 'VALID', dimension_numbers...  27.7 us
    unnamed x10, local copies, waits for them, and re-layouts  8.67 us
    mul x2, local copies, waits for them, and re-layouts, correlate(): return result * score_scale  4.91 us
  transfers between devices with their start and end apart: 3, of which 3 were waited for; matrix products, arithmetic and copies ran while one was open for 2% of the time, Pallas kernels for 0%

commit v1 on v0

v1 whole, which is shorter than its diff:
```python
import functools

import jax
import jax.numpy as jnp
from jax import lax
from jax.experimental import pallas as pl
from jax.experimental.pallas import tpu as pltpu
from jax.sharding import PartitionSpec as P

RECS = 16
SHIFTS = 16
ROWS = 512
PIECE = 64
LOW = -1e30
MESH = pl.DeviceIdType.MESH


def kernel(
    n, n_tm, score_scale,
    corpus, bank, meta, rec_out, top_out,
    frames, wide, unfolded, weights, scores, ids, rim_ids, bias, labels,
    piece_max, piece_sum, stats, slabs, group, groups_all,
    local_sem, send_sem, recv_sem,
):
    i, z, c = lax.axis_index("tmpl"), lax.axis_index("tm"), lax.axis_index("rec")
    parity = lax.rem(i, 2)
    side = i + 1 - 2 * parity
    rows = bank.shape[0]
    length = corpus.shape[0]
    halo = frames.shape[1] - length
    chunks = weights.shape[0]
    depth = weights.shape[2]
    cols = weights.shape[1]
    id_rows = length // 128
    half = n // 2

    def at(j, zz, cc):
        return {"tmpl": j, "tm": zz, "rec": cc}

    def tmpl_plus(by):
        return lax.rem(i + by + n, n)

    def tm_plus(by):
        return lax.rem(z + by + n_tm, n_tm)

    slots = {}

    def slot(name):
        return slots.setdefault(name, len(slots))

    def remote(name, src, dst, device):
        k = slot(name)
        return pltpu.make_async_remote_copy(
            src_ref=src, dst_ref=dst, send_sem=send_sem.at[k], recv_sem=recv_sem.at[k],
            device_id=device, device_id_type=MESH,
        )

    def block(q, j, cc):
        shard = (j // 2) * 2 + cc
        return weights.at[q, pl.ds(pl.multiple_of(shard * rows, 16), rows)]

    own_frames = pltpu.make_async_copy(corpus, frames.at[0, pl.ds(0, length)], local_sem.at[0])
    own_meta = pltpu.make_async_copy(meta, ids.at[0], local_sem.at[1])
    own_frames.start()
    own_meta.start()
    own_bank = []
    for q in range(chunks):
        own_bank.append(pltpu.make_async_copy(
            bank.at[:, pl.ds(q * depth, depth)], block(q, i, c), local_sem.at[2 + q]))
        own_bank[-1].start()

    barrier = pltpu.get_barrier_semaphore()
    partners = [at(tmpl_plus(dj), z, c if dc == 0 else 1 - c)
                for dj in range(n) for dc in range(2) if dj or dc]
    for dz in range(1, n_tm):
        partners += [at(i, tm_plus(dz), c), at(side, tm_plus(dz), c)]
    for device in partners:
        pl.semaphore_signal(barrier, inc=1, device_id=device, device_id_type=MESH)
    pl.semaphore_wait(barrier, len(partners))

    sent = []

    def start(copy):
        copy.start()
        sent.append(copy)

    rim = corpus.at[pl.ds(0, halo)]
    rim_meta = meta.at[pl.ds(0, 8)]
    before, after = tm_plus(-1), tm_plus(1)
    rim_copies = []
    for g, j in ((0, i), (1, side)):
        rim_copies.append(remote(("rim", g), rim, frames.at[g, pl.ds(length, halo)], at(j, before, c)))
        rim_copies.append(remote(("rim_ids", g), rim_meta, rim_ids.at[g], at(j, before, c)))

    @pl.when(z > 0)
    def _():
        for copy in rim_copies:
            copy.start()

    @pl.when(z == n_tm - 1)
    def _():
        for g in range(2):
            frames[g, pl.ds(length, halo), :] = jnp.zeros((halo, frames.shape[2]), jnp.bfloat16)
            rim_ids[g] = jnp.full(rim_ids.shape[1:], -1, jnp.int32)

    side_meta = remote("meta", meta, ids.at[1], at(side, z, c))
    start(side_meta)
    side_frames = remote("frames", corpus, frames.at[1, pl.ds(0, length)], at(side, z, c))
    for q in range(chunks):
        part = bank.at[:, pl.ds(q * depth, depth)]
        for d in range(1, half):
            start(remote(("bank", q, d), part, block(q, i, c), at(tmpl_plus(2 * d), z, c)))
        start(remote(("core", q), part, block(q, i, c), at(i, z, 1 - c)))
        if q == 0:
            start(side_frames)

    def arrive_bank(q):
        for d in range(1, half):
            j = tmpl_plus(-2 * d)
            remote(("bank", q, d), block(q, j, c), block(q, j, c), at(j, z, c)).wait_recv()
            start(remote(("pass", q, d), block(q, j, c), block(q, j, c), at(i, z, 1 - c)))

    def finish_bank(q):
        own_bank[q].wait()
        here = block(q, i, 1 - c)
        remote(("core", q), here, here, at(i, z, 1 - c)).wait_recv()
        for d in range(1, half):
            there = block(q, tmpl_plus(-2 * d), 1 - c)
            remote(("pass", q, d), there, there, at(i, z, 1 - c)).wait_recv()

    def unfold(g):
        @pl.when(z < n_tm - 1)
        def _():
            rim_copies[2 * g].wait_recv()
            rim_copies[2 * g + 1].wait_recv()

        total = length + halo
        wide[pl.ds(total, SHIFTS), :] = jnp.zeros((SHIFTS, wide.shape[1]), jnp.float32)

        @pl.loop(0, total // 64)
        def _(step):
            here = pl.ds(pl.multiple_of(step * 64, 64), 64)
            wide[here, :] = frames[g, here, :].astype(jnp.float32)

        @pl.loop(0, total // 64)
        def _(step):
            base = pl.multiple_of(step * 64, 64)
            for s in range(SHIFTS):
                unfolded[g, pl.ds(base, 64), s * 128:(s + 1) * 128] = (
                    wide[pl.ds(base + s, 64), :].astype(jnp.bfloat16))

        now = ids[g, 0:id_rows, :]
        rolled = pltpu.roll(now, 128 - (PIECE - 1), 1)
        rolled_rim = pltpu.roll(rim_ids[g], 128 - (PIECE - 1), 1)
        next_row = jnp.concatenate([rolled[1:], rolled_rim[0:1]], axis=0)
        lane = lax.broadcasted_iota(jnp.int32, now.shape, 1)
        row = lax.broadcasted_iota(jnp.int32, now.shape, 0)
        last = jnp.where(lane < 128 - (PIECE - 1), rolled, next_row)
        valid = ids[g, id_rows:id_rows + 1, :]
        usable = (now == last) & (row * 128 + lane < valid)
        flat = jnp.where(usable, 0.0, LOW)
        flat = jnp.concatenate([flat, jnp.zeros((128 - id_rows, 128), jnp.float32)], axis=0)
        turned = flat.T
        for r in range(id_rows):
            bias[g, r * 128:(r + 1) * 128, :] = jnp.broadcast_to(turned[:, r:r + 1], (128, 128))
        named = jnp.where(usable, now, -1)
        first = jnp.max(jnp.where(lane < PIECE, named, -1), axis=1, keepdims=True)
        second = jnp.max(jnp.where(lane >= PIECE, named, -1), axis=1, keepdims=True)
        labels[g, 0:id_rows, :] = jnp.broadcast_to(first, (id_rows, 128))
        labels[g, id_rows:2 * id_rows, :] = jnp.broadcast_to(second, (id_rows, 128))

    def correlate(g, q):
        @pl.loop(0, length // ROWS)
        def _(step):
            base = pl.multiple_of(step * ROWS, ROWS)
            part = lax.dot_general(
                unfolded[g, pl.ds(pl.multiple_of(base + q * SHIFTS, SHIFTS), ROWS), :], weights[q],
                (((1,), (1,)), ((), ())), preferred_element_type=jnp.float32)
            if q == 0:
                scores[g, pl.ds(base, ROWS), :] = part
            else:
                scores[g, pl.ds(base, ROWS), :] += part

    def summarize(g):
        @pl.loop(0, id_rows)
        def _(r):
            for h in range(2):
                base = pl.multiple_of(r * 128 + h * PIECE, PIECE)
                mask = bias[g, pl.ds(base, PIECE), :]
                for k in range(0, cols, 128):
                    x = scores[g, pl.ds(base, PIECE), k:k + 128] * score_scale + mask
                    top = jnp.maximum(jnp.max(x, axis=0, keepdims=True), 0.0)
                    piece_max[k // 128, pl.ds(h * id_rows + r, 1), :] = top
                    piece_sum[k // 128, pl.ds(h * id_rows + r, 1), :] = jnp.sum(
                        jnp.exp(x - top), axis=0, keepdims=True)

        name = jnp.concatenate([labels[g]] * (cols // 128), axis=1)
        tops = jnp.concatenate([piece_max[k] for k in range(cols // 128)], axis=1)
        sums = jnp.concatenate([piece_sum[k] for k in range(cols // 128)], axis=1)
        for r in range(RECS):
            mine = name == r
            peak = jnp.max(jnp.where(mine, tops, 0.0), axis=0, keepdims=True)
            total = jnp.sum(jnp.where(mine, sums * jnp.exp(jnp.minimum(tops - peak, 0.0)), 0.0), axis=0, keepdims=True)
            stats[g, r:r + 1, :] = peak
            stats[g, RECS + r:RECS + r + 1, :] = total

    own_frames.wait()
    own_meta.wait()
    unfold(0)
    arrive_bank(0)
    finish_bank(0)
    for q in range(chunks - 1):
        correlate(0, q)
        arrive_bank(q + 1)
        if q == 0:
            side_frames.wait_recv()
            side_meta.wait_recv()
            unfold(1)
        correlate(1, q)
        finish_bank(q + 1)
    correlate(1, chunks - 1)
    summarize(1)
    for dz in range(n_tm):
        start(remote(("side", dz), stats.at[1], slabs.at[z, parity], at(side, tm_plus(dz), c)))
    correlate(0, chunks - 1)
    summarize(0)
    for dz in range(1, n_tm):
        start(remote(("own", dz), stats.at[0], slabs.at[z, parity], at(i, tm_plus(dz), c)))
    slabs[z, parity] = stats[0]
    for dz in range(n_tm):
        there = slabs.at[tm_plus(-dz), 1 - parity]
        remote(("side", dz), there, there, at(side, z, c)).wait_recv()
    for dz in range(1, n_tm):
        there = slabs.at[tm_plus(-dz), parity]
        remote(("own", dz), there, there, at(i, tm_plus(-dz), c)).wait_recv()

    for h in range(2):
        peak = slabs[0, h, 0:RECS, :]
        for s in range(1, n_tm):
            peak = jnp.maximum(peak, slabs[s, h, 0:RECS, :])
        total = jnp.zeros_like(peak)
        for s in range(n_tm):
            total += slabs[s, h, RECS:2 * RECS, :] * jnp.exp(slabs[s, h, 0:RECS, :] - peak)
        rec_out[h] = peak + jnp.log(jnp.exp(-peak) + total)
        top = jnp.max(peak, axis=0, keepdims=True)
        group[2 * h:2 * h + 1, :] = top
        group[2 * h + 1:2 * h + 2, :] = jnp.sum(total * jnp.exp(peak - top), axis=0, keepdims=True)
    group[4:8, :] = jnp.zeros((4, cols), jnp.float32)

    mine = 2 * i + c
    for dj in range(n):
        for dc in range(2):
            if dj or dc:
                start(remote(("group", dj, dc), group, groups_all.at[mine],
                             at(tmpl_plus(dj), z, c if dc == 0 else 1 - c)))
    groups_all[mine] = group[...]
    for dj in range(n):
        for dc in range(2):
            if dj or dc:
                there = groups_all.at[2 * tmpl_plus(-dj) + (c if dc == 0 else 1 - c)]
                remote(("group", dj, dc), there, there, at(tmpl_plus(-dj), z, c if dc == 0 else 1 - c)).wait_recv()
    for h in range(2):
        top = groups_all[0, 2 * h:2 * h + 1, :]
        for s in range(1, 2 * n):
            top = jnp.maximum(top, groups_all[s, 2 * h:2 * h + 1, :])
        total = jnp.zeros_like(top)
        for s in range(2 * n):
            total += groups_all[s, 2 * h + 1:2 * h + 2, :] * jnp.exp(groups_all[s, 2 * h:2 * h + 1, :] - top)
        top_out[h:h + 1, :] = top + jnp.log(jnp.exp(-top) + total)

    for copy in sent:
        copy.wait_send()

    @pl.when(z > 0)
    def _():
        for copy in rim_copies:
            copy.wait_send()


def on_device(n, n_tm, corpus, templates, rec_ids, valid_frames):
    rows, span, bins = templates.shape
    length = corpus.shape[1]
    halo = span
    id_rows = length // 128
    chunks = span // SHIFTS
    depth = SHIFTS * bins
    cols = rows * n
    meta = jnp.concatenate(
        [rec_ids.reshape(id_rows, 128), jnp.broadcast_to(valid_frames.reshape(1, 1), (8, 128))], axis=0)
    copies = 5 + chunks * n + 2 * n_tm + 2 * n
    f32, bf16, i32 = jnp.float32, jnp.bfloat16, jnp.int32
    rec_half, top_half = pl.pallas_call(
        functools.partial(kernel, n, n_tm, (span * bins) ** (-0.5)),
        out_shape=(jax.ShapeDtypeStruct((2, RECS, cols), f32), jax.ShapeDtypeStruct((2, cols), f32)),
        in_specs=[pl.BlockSpec(memory_space=pl.ANY)] * 3,
        out_specs=(pl.BlockSpec(memory_space=pltpu.VMEM), pl.BlockSpec(memory_space=pltpu.VMEM)),
        scratch_shapes=[
            pltpu.VMEM((2, length + halo, bins), bf16),
            pltpu.VMEM((length + halo + SHIFTS, bins), f32),
            pltpu.VMEM((2, length + halo, depth), bf16),
            pltpu.VMEM((chunks, cols, depth), bf16),
            pltpu.VMEM((2, length, cols), f32),
            pltpu.VMEM((2, id_rows + 8, 128), i32),
            pltpu.VMEM((2, 8, 128), i32),
            pltpu.VMEM((2, length, 128), f32),
            pltpu.VMEM((2, 2 * id_rows, 128), i32),
            pltpu.VMEM((cols // 128, 2 * id_rows, 128), f32),
            pltpu.VMEM((cols // 128, 2 * id_rows, 128), f32),
            pltpu.VMEM((2, 2 * RECS, cols), f32),
            pltpu.VMEM((n_tm, 2, 2 * RECS, cols), f32),
            pltpu.VMEM((8, cols), f32),
            pltpu.VMEM((2 * n, 8, cols), f32),
            pltpu.SemaphoreType.DMA((2 + chunks,)),
            pltpu.SemaphoreType.DMA((copies,)),
            pltpu.SemaphoreType.DMA((copies,)),
        ],
        compiler_params=pltpu.CompilerParams(
            collective_id=0, has_side_effects=True, vmem_limit_bytes=48 * 1024 * 1024),
    )(corpus[0], templates.reshape(rows, span * bins), meta)
    rec = rec_half.reshape(2, RECS, n // 2, 2 * rows).transpose(1, 2, 0, 3).reshape(1, RECS, n * 2 * rows)
    top = top_half.reshape(2, n // 2, 2 * rows).transpose(1, 0, 2).reshape(n * 2 * rows)
    return rec, top


def solution(mesh):
    return jax.shard_map(
        functools.partial(on_device, mesh.shape["tmpl"], mesh.shape["tm"]),
        mesh=mesh,
        in_specs=(
            P(("tmpl", "rec"), "tm", None),
            P(("tmpl", "rec"), None, None),
            P(("tmpl", "rec"), "tm"),
            P(("tmpl", "rec"), "tm"),
        ),
        out_specs=(P(("tmpl", "rec"), None, None), P()),
        check_vma=False,
    )
```

time: 206 us -> 57.9 us (0.28)
  Pallas kernels: 0 us -> 53 us
  waiting for transfers between devices: 49.8 us -> 0 us
  other arithmetic: 46.3 us -> 0 us
  blocking collectives: 43.6 us -> 0 us
  matrix products: 32.1 us -> 0 us
  between operations: 14.8 us -> 1.33 us
  local copies, waits for them, and re-layouts: 15.4 us -> 3.28 us
  starting transfers between devices: 2.6 us -> 0 us
    pallas_call x0 -> x1, Pallas kernels: none -> 53 us  [on_device(): pl.pallas_call(functools.partial(kernel, n, n_tm, (span * bins) ** (-0.5)...]
    all_gather x1 -> x0, waiting for transfers between devices: 46 us -> none  [on_device(): lax.all_gather(templates, ('tmpl', 'rec'), axis=0, tiled=True)]
    all_gather x4 -> x0, blocking collectives: 43.6 us -> none  [merged(): gathered = jax.tree.map(lambda a: lax.all_gather(a, axis), part)]
    reduce_max x17 -> x0, other arithmetic: 40.7 us -> none  [the longest x16 40.7 us: top_of(): return jnp.max(jnp.where(label_row[None, :] > 0, scores, -jnp.inf), axis=1)]
    conv_general_dilated x1 -> x0, matrix products: 27.7 us -> none  [correlate(): lax.conv_general_dilated(extended, bank, (1,), 'VALID', dimension_numbers...]
    unnamed x10 -> x6, local copies, waits for them, and re-layouts: 8.67 us -> 2.59 us
    mul x2 -> x0, local copies, waits for them, and re-layouts: 4.91 us -> none  [correlate(): return result * score_scale]
    dot_general x2 -> x0, matrix products: 4.39 us -> none  [the longest x1 2.53 us: slab_stats(): totals = jnp.dot(member, weights.T, precision=lax.Precision.HIGHEST)]
  transfers between devices with their start and end apart: 3 -> 0, of which waited for: 3 -> 0; matrix products, arithmetic and copies ran while one was open for 2% -> 0% of each run, Pallas kernels for 0% -> 0%
where the time goes in v1:
time: 57.9 us; the launch traced here: 57.6 us
  Pallas kernels  53 us (92%)
  local copies, waits for them, and re-layouts  3.28 us (6%)
  between operations  1.33 us (2%)
    pallas_call x1, Pallas kernels, on_device(): pl.pallas_call(functools.partial(kernel, n, n_tm, (span * bins) ** (-0.5)...  53 us
    unnamed x6, local copies, waits for them, and re-layouts  2.59 us

profile of v1, /device:TPU:0, one launch (start us, length us, event | category | flops | bytes accessed | tf_op | source)
XLA Modules:
  0.0 57.6 jit_solution(13537201230357857272)
XLA Ops:
  0.6 0.0 copy-start.1
  1.3 0.0 copy-done.1
  1.3 0.0 copy-start
  1.3 2.0 %copy.11 = bf16[8,8,64,128]{3,1,2,0:T(8,128)(2,1)S(1)} copy(bf16[8,8,64,128]{3,2,1,0:T(8,128)(2,1)} %bitcast.17) | data formatting | bytes 2097152
  3.3 0.0 copy-done
  3.3 53.0 %shard_map.59 = (f32[2,16,256]{2,1,0:T(8,128)S(1)}, f32[2,256]{1,0:T(2,128)S(1)}) custom-call(bf16[2048,128]{1,0:T(8,128)(2,1)S(1)} %bitcast.15, bf16[64,8192]{1,0:T(8,128)(2,1)S(1)} %bitcast.14, s32[24,128]{1,0:T(8,128)S(1)} %concatenate.3.meta), custom_call_target="tpu_custom_call" | custom-call | tf_op jit(solution)/shard_map/pallas_call | solution.py:292
  56.4 0.6 %reshape.25 = f32[1,16,512]{2,1,0:T(8,128)} reshape(f32[16,2,2,128]{3,2,1,0:T(2,128)S(1)} %copy.7) | data formatting | bytes 65536 | tf_op jit(solution)/shard_map/reshape | solution.py:320
  57.1 0.6 %copy.14 = f32[512]{0:T(512)} copy(f32[512]{0:T(512)S(1)} %bitcast.16) | data formatting | bytes 4096
  (3 shorter events, 0.0 us)
Async XLA Ops:
  0.6 0.7 %copy-start.1 = (s32[1,2048]{1,0:T(1,128)S(1)}, s32[1,2048]{1,0:T(1,128)}, u32[]{:S(2)}) copy-start(s32[1,2048]{1,0:T(1,128)} %param.6) | copy-start | bytes 24580
  1.3 2.0 %copy-start = (bf16[1,2048,128]{2,1,0:T(8,128)(2,1)S(1)}, bf16[1,2048,128]{2,1,0:T(8,128)(2,1)}, u32[]{:S(2)}) copy-start(bf16[1,2048,128]{2,1,0:T(8,128)(2,1)} %param.4) | copy-start | bytes 1572868

commit v2 on v1

--- a/solution.py
+++ b/solution.py
@@ -9,7 +9,8 @@
 
 RECS = 16
 SHIFTS = 16
-ROWS = 512
+HALF = 8
+ROWS = 1024
 PIECE = 64
 LOW = -1e30
 MESH = pl.DeviceIdType.MESH
@@ -33,6 +34,8 @@
     cols = weights.shape[1]
     id_rows = length // 128
     half = n // 2
+    near = z + 1 - 2 * lax.rem(z, 2)
+    mine_half = lax.rem(z, 2)
 
     def at(j, zz, cc):
         return {"tmpl": j, "tm": zz, "rec": cc}
@@ -58,6 +61,10 @@
     def block(q, j, cc):
         shard = (j // 2) * 2 + cc
         return weights.at[q, pl.ds(pl.multiple_of(shard * rows, 16), rows)]
+
+    def half_block(q, j, cc, which):
+        first = ((j // 2) * 2 + cc) * rows + which * (rows // 2)
+        return weights.at[q, pl.ds(pl.multiple_of(first, 16), rows // 2)]
 
     own_frames = pltpu.make_async_copy(corpus, frames.at[0, pl.ds(0, length)], local_sem.at[0])
     own_meta = pltpu.make_async_copy(meta, ids.at[0], local_sem.at[1])
@@ -107,26 +114,38 @@
     start(side_meta)
     side_frames = remote("frames", corpus, frames.at[1, pl.ds(0, length)], at(side, z, c))
     for q in range(chunks):
-        part = bank.at[:, pl.ds(q * depth, depth)]
+        own_half = bank.at[pl.ds(pl.multiple_of(mine_half * (rows // 2), 16), rows // 2), pl.ds(q * depth, depth)]
         for d in range(1, half):
-            start(remote(("bank", q, d), part, block(q, i, c), at(tmpl_plus(2 * d), z, c)))
-        start(remote(("core", q), part, block(q, i, c), at(i, z, 1 - c)))
+            start(remote(("bank", q, d), own_half, half_block(q, i, c, mine_half), at(tmpl_plus(2 * d), z, c)))
+        start(remote(("core", q), bank.at[:, pl.ds(q * depth, depth)], block(q, i, c), at(i, z, 1 - c)))
         if q == 0:
             start(side_frames)
 
-    def arrive_bank(q):
+    def arrive(q):
+        if q >= chunks:
+            return
         for d in range(1, half):
-            j = tmpl_plus(-2 * d)
-            remote(("bank", q, d), block(q, j, c), block(q, j, c), at(j, z, c)).wait_recv()
-            start(remote(("pass", q, d), block(q, j, c), block(q, j, c), at(i, z, 1 - c)))
-
-    def finish_bank(q):
+            there = half_block(q, tmpl_plus(-2 * d), c, mine_half)
+            remote(("bank", q, d), there, there, at(i, near, c)).wait_recv()
+            start(remote(("near", q, d), there, there, at(i, near, c)))
+            start(remote(("pass", q, d, 0), there, there, at(i, z, 1 - c)))
+
+    def arrive_near(q):
+        if q >= chunks:
+            return
+        for d in range(1, half):
+            there = half_block(q, tmpl_plus(-2 * d), c, 1 - mine_half)
+            remote(("near", q, d), there, there, at(i, near, c)).wait_recv()
+            start(remote(("pass", q, d, 1), there, there, at(i, z, 1 - c)))
+
+    def finish(q):
         own_bank[q].wait()
         here = block(q, i, 1 - c)
         remote(("core", q), here, here, at(i, z, 1 - c)).wait_recv()
         for d in range(1, half):
-            there = block(q, tmpl_plus(-2 * d), 1 - c)
-            remote(("pass", q, d), there, there, at(i, z, 1 - c)).wait_recv()
+            for k, which in ((0, mine_half), (1, 1 - mine_half)):
+                there = half_block(q, tmpl_plus(-2 * d), 1 - c, which)
+                remote(("pass", q, d, k), there, there, at(i, z, 1 - c)).wait_recv()
 
     def unfold(g):
         @pl.when(z < n_tm - 1)
@@ -169,17 +188,33 @@
         labels[g, 0:id_rows, :] = jnp.broadcast_to(first, (id_rows, 128))
         labels[g, id_rows:2 * id_rows, :] = jnp.broadcast_to(second, (id_rows, 128))
 
-    def correlate(g, q):
+    def correlate(q):
+        first = q * HALF // SHIFTS * SHIFTS
+        lanes = slice(q * depth % unfolded.shape[2], q * depth % unfolded.shape[2] + depth)
+        part = lax.dot_general(
+            unfolded[0, first:first + length, lanes], weights[q],
+            (((1,), (1,)), ((), ())), preferred_element_type=jnp.float32)
+        if q == 0:
+            scores[0] = part
+        else:
+            scores[0] += part
+
+    def correlate_all(g):
         @pl.loop(0, length // ROWS)
         def _(step):
             base = pl.multiple_of(step * ROWS, ROWS)
-            part = lax.dot_general(
-                unfolded[g, pl.ds(pl.multiple_of(base + q * SHIFTS, SHIFTS), ROWS), :], weights[q],
-                (((1,), (1,)), ((), ())), preferred_element_type=jnp.float32)
-            if q == 0:
-                scores[g, pl.ds(base, ROWS), :] = part
-            else:
-                scores[g, pl.ds(base, ROWS), :] += part
+            total = None
+            for q in range(chunks):
+                first = q * HALF // SHIFTS * SHIFTS
+                lanes = slice(q * depth % unfolded.shape[2], q * depth % unfolded.shape[2] + depth)
+                part = lax.dot_general(
+                    unfolded[g, pl.ds(pl.multiple_of(base + first, SHIFTS), ROWS), lanes], weights[q],
+                    (((1,), (1,)), ((), ())), preferred_element_type=jnp.float32)
+                total = part if total is None else total + part
+            scores[g, pl.ds(base, ROWS), :] = total
+
+    def log_of(peak, total):
+        return jnp.where(total > 0.0, peak + jnp.log(total), LOW)
 
     def summarize(g):
         @pl.loop(0, id_rows)
@@ -201,31 +236,33 @@
             mine = name == r
             peak = jnp.max(jnp.where(mine, tops, 0.0), axis=0, keepdims=True)
             total = jnp.sum(jnp.where(mine, sums * jnp.exp(jnp.minimum(tops - peak, 0.0)), 0.0), axis=0, keepdims=True)
-            stats[g, r:r + 1, :] = peak
-            stats[g, RECS + r:RECS + r + 1, :] = total
+            stats[g, r:r + 1, :] = log_of(peak, total)
 
     own_frames.wait()
     own_meta.wait()
     unfold(0)
-    arrive_bank(0)
-    finish_bank(0)
-    for q in range(chunks - 1):
-        correlate(0, q)
-        arrive_bank(q + 1)
-        if q == 0:
-            side_frames.wait_recv()
-            side_meta.wait_recv()
-            unfold(1)
-        correlate(1, q)
-        finish_bank(q + 1)
-    correlate(1, chunks - 1)
+    arrive(0)
+    arrive(1)
+    arrive_near(0)
+    arrive(2)
+    arrive_near(1)
+    finish(0)
+    for q in range(chunks):
+        correlate(q)
+        arrive(q + 3)
+        arrive_near(q + 2)
+        if q + 1 < chunks:
+            finish(q + 1)
+    summarize(0)
+    for dz in range(1, n_tm):
+        start(remote(("own", dz), stats.at[0], slabs.at[z, parity], at(i, tm_plus(dz), c)))
+    side_frames.wait_recv()
+    side_meta.wait_recv()
+    unfold(1)
+    correlate_all(1)
     summarize(1)
     for dz in range(n_tm):
         start(remote(("side", dz), stats.at[1], slabs.at[z, parity], at(side, tm_plus(dz), c)))
-    correlate(0, chunks - 1)
-    summarize(0)
-    for dz in range(1, n_tm):
-        start(remote(("own", dz), stats.at[0], slabs.at[z, parity], at(i, tm_plus(dz), c)))
     slabs[z, parity] = stats[0]
     for dz in range(n_tm):
         there = slabs.at[tm_plus(-dz), 1 - parity]
@@ -235,17 +272,16 @@
         remote(("own", dz), there, there, at(i, tm_plus(-dz), c)).wait_recv()
 
     for h in range(2):
-        peak = slabs[0, h, 0:RECS, :]
+        peak = jnp.maximum(slabs[0, h], 0.0)
         for s in range(1, n_tm):
-            peak = jnp.maximum(peak, slabs[s, h, 0:RECS, :])
+            peak = jnp.maximum(peak, slabs[s, h])
         total = jnp.zeros_like(peak)
         for s in range(n_tm):
-            total += slabs[s, h, RECS:2 * RECS, :] * jnp.exp(slabs[s, h, 0:RECS, :] - peak)
+            total += jnp.exp(slabs[s, h] - peak)
         rec_out[h] = peak + jnp.log(jnp.exp(-peak) + total)
         top = jnp.max(peak, axis=0, keepdims=True)
-        group[2 * h:2 * h + 1, :] = top
-        group[2 * h + 1:2 * h + 2, :] = jnp.sum(total * jnp.exp(peak - top), axis=0, keepdims=True)
-    group[4:8, :] = jnp.zeros((4, cols), jnp.float32)
+        group[h:h + 1, :] = log_of(top, jnp.sum(total * jnp.exp(peak - top), axis=0, keepdims=True))
+    group[2:8, :] = jnp.zeros((6, cols), jnp.float32)
 
     mine = 2 * i + c
     for dj in range(n):
@@ -259,14 +295,13 @@
             if dj or dc:
                 there = groups_all.at[2 * tmpl_plus(-dj) + (c if dc == 0 else 1 - c)]
                 remote(("group", dj, dc), there, there, at(tmpl_plus(-dj), z, c if dc == 0 else 1 - c)).wait_recv()
-    for h in range(2):
-        top = groups_all[0, 2 * h:2 * h + 1, :]
-        for s in range(1, 2 * n):
-            top = jnp.maximum(top, groups_all[s, 2 * h:2 * h + 1, :])
-        total = jnp.zeros_like(top)
-        for s in range(2 * n):
-            total += groups_all[s, 2 * h + 1:2 * h + 2, :] * jnp.exp(groups_all[s, 2 * h:2 * h + 1, :] - top)
-        top_out[h:h + 1, :] = top + jnp.log(jnp.exp(-top) + total)
+    top = jnp.maximum(groups_all[0, 0:2, :], 0.0)
+    for s in range(1, 2 * n):
+        top = jnp.maximum(top, groups_all[s, 0:2, :])
+    total = jnp.zeros_like(top)
+    for s in range(2 * n):
+        total += jnp.exp(groups_all[s, 0:2, :] - top)
+    top_out[...] = top + jnp.log(jnp.exp(-top) + total)
 
     for copy in sent:
         copy.wait_send()
@@ -282,12 +317,12 @@
     length = corpus.shape[1]
     halo = span
     id_rows = length // 128
-    chunks = span // SHIFTS
-    depth = SHIFTS * bins
+    chunks = span // HALF
+    depth = HALF * bins
     cols = rows * n
     meta = jnp.concatenate(
         [rec_ids.reshape(id_rows, 128), jnp.broadcast_to(valid_frames.reshape(1, 1), (8, 128))], axis=0)
-    copies = 5 + chunks * n + 2 * n_tm + 2 * n
+    copies = 6 + chunks * 2 * n + 2 * n_tm + 2 * n
     f32, bf16, i32 = jnp.float32, jnp.bfloat16, jnp.int32
     rec_half, top_half = pl.pallas_call(
         functools.partial(kernel, n, n_tm, (span * bins) ** (-0.5)),
@@ -297,7 +332,7 @@
         scratch_shapes=[
             pltpu.VMEM((2, length + halo, bins), bf16),
             pltpu.VMEM((length + halo + SHIFTS, bins), f32),
-            pltpu.VMEM((2, length + halo, depth), bf16),
+            pltpu.VMEM((2, length + halo, SHIFTS * bins), bf16),
             pltpu.VMEM((chunks, cols, depth), bf16),
             pltpu.VMEM((2, length, cols), f32),
             pltpu.VMEM((2, id_rows + 8, 128), i32),
@@ -306,8 +341,8 @@
             pltpu.VMEM((2, 2 * id_rows, 128), i32),
             pltpu.VMEM((cols // 128, 2 * id_rows, 128), f32),
             pltpu.VMEM((cols // 128, 2 * id_rows, 128), f32),
-            pltpu.VMEM((2, 2 * RECS, cols), f32),
-            pltpu.VMEM((n_tm, 2, 2 * RECS, cols), f32),
+            pltpu.VMEM((2, RECS, cols), f32),
+            pltpu.VMEM((n_tm, 2, RECS, cols), f32),
             pltpu.VMEM((8, cols), f32),
             pltpu.VMEM((2 * n, 8, cols), f32),
             pltpu.SemaphoreType.DMA((2 + chunks,)),

time: 57.9 us -> 65 us (1.12)
  Pallas kernels: 53 us -> 60.2 us
    pallas_call x1, Pallas kernels: 53 us -> 60.2 us  [on_device(): pl.pallas_call(functools.partial(kernel, n, n_tm, (span * bins) ** (-0.5)...]
where the time goes in v2:
time: 65 us; the launch traced here: 64.8 us
  Pallas kernels  60.2 us (93%)
  local copies, waits for them, and re-layouts  3.28 us (5%)
  between operations  1.33 us (2%)
    pallas_call x1, Pallas kernels, on_device(): pl.pallas_call(functools.partial(kernel, n, n_tm, (span * bins) ** (-0.5)...  60.2 us
    unnamed x6, local copies, waits for them, and re-layouts  2.59 us

profile of v2, /device:TPU:0, one launch (start us, length us, event | category | flops | bytes accessed | tf_op | source)
XLA Modules:
  0.0 64.8 jit_solution(14834806961879988174)
XLA Ops:
  0.6 0.0 copy-start.1
  1.3 0.0 copy-done.1
  1.3 0.0 copy-start
  1.3 2.0 %copy.11 = bf16[8,8,64,128]{3,1,2,0:T(8,128)(2,1)S(1)} copy(bf16[8,8,64,128]{3,2,1,0:T(8,128)(2,1)} %bitcast.17) | data formatting | bytes 2097152
  3.3 0.0 copy-done
  3.3 60.2 %shard_map.59 = (f32[2,16,256]{2,1,0:T(8,128)S(1)}, f32[2,256]{1,0:T(2,128)S(1)}) custom-call(bf16[2048,128]{1,0:T(8,128)(2,1)S(1)} %bitcast.15, bf16[64,8192]{1,0:T(8,128)(2,1)S(1)} %bitcast.14, s32[24,128]{1,0:T(8,128)S(1)} %concatenate.3.meta), custom_call_target="tpu_custom_call" | custom-call | tf_op jit(solution)/shard_map/pallas_call | solution.py:327
  63.6 0.6 reshape.25
  64.2 0.6 copy.14
  (3 shorter events, 0.0 us)
Async XLA Ops:
  0.6 0.7 %copy-start.1 = (s32[1,2048]{1,0:T(1,128)S(1)}, s32[1,2048]{1,0:T(1,128)}, u32[]{:S(2)}) copy-start(s32[1,2048]{1,0:T(1,128)} %param.6) | copy-start | bytes 24580
  1.3 2.0 %copy-start = (bf16[1,2048,128]{2,1,0:T(8,128)(2,1)S(1)}, bf16[1,2048,128]{2,1,0:T(8,128)(2,1)}, u32[]{:S(2)}) copy-start(bf16[1,2048,128]{2,1,0:T(8,128)(2,1)} %param.4) | copy-start | bytes 1572868

commit v3 on v2

--- a/solution.py
+++ b/solution.py
@@ -34,8 +34,6 @@
     cols = weights.shape[1]
     id_rows = length // 128
     half = n // 2
-    near = z + 1 - 2 * lax.rem(z, 2)
-    mine_half = lax.rem(z, 2)
 
     def at(j, zz, cc):
         return {"tmpl": j, "tm": zz, "rec": cc}
@@ -62,9 +60,13 @@
         shard = (j // 2) * 2 + cc
         return weights.at[q, pl.ds(pl.multiple_of(shard * rows, 16), rows)]
 
-    def half_block(q, j, cc, which):
-        first = ((j // 2) * 2 + cc) * rows + which * (rows // 2)
-        return weights.at[q, pl.ds(pl.multiple_of(first, 16), rows // 2)]
+    barrier = pltpu.get_barrier_semaphore()
+    partners = [at(tmpl_plus(dj), z, c if dc == 0 else 1 - c)
+                for dj in range(n) for dc in range(2) if dj or dc]
+    for dz in range(1, n_tm):
+        partners += [at(i, tm_plus(dz), c), at(side, tm_plus(dz), c)]
+    for device in partners:
+        pl.semaphore_signal(barrier, inc=1, device_id=device, device_id_type=MESH)
 
     own_frames = pltpu.make_async_copy(corpus, frames.at[0, pl.ds(0, length)], local_sem.at[0])
     own_meta = pltpu.make_async_copy(meta, ids.at[0], local_sem.at[1])
@@ -76,13 +78,6 @@
             bank.at[:, pl.ds(q * depth, depth)], block(q, i, c), local_sem.at[2 + q]))
         own_bank[-1].start()
 
-    barrier = pltpu.get_barrier_semaphore()
-    partners = [at(tmpl_plus(dj), z, c if dc == 0 else 1 - c)
-                for dj in range(n) for dc in range(2) if dj or dc]
-    for dz in range(1, n_tm):
-        partners += [at(i, tm_plus(dz), c), at(side, tm_plus(dz), c)]
-    for device in partners:
-        pl.semaphore_signal(barrier, inc=1, device_id=device, device_id_type=MESH)
     pl.semaphore_wait(barrier, len(partners))
 
     sent = []
@@ -113,39 +108,34 @@
     side_meta = remote("meta", meta, ids.at[1], at(side, z, c))
     start(side_meta)
     side_frames = remote("frames", corpus, frames.at[1, pl.ds(0, length)], at(side, z, c))
-    for q in range(chunks):
-        own_half = bank.at[pl.ds(pl.multiple_of(mine_half * (rows // 2), 16), rows // 2), pl.ds(q * depth, depth)]
+    def send_bank(q):
+        if q >= chunks:
+            return
+        part = bank.at[:, pl.ds(q * depth, depth)]
         for d in range(1, half):
-            start(remote(("bank", q, d), own_half, half_block(q, i, c, mine_half), at(tmpl_plus(2 * d), z, c)))
-        start(remote(("core", q), bank.at[:, pl.ds(q * depth, depth)], block(q, i, c), at(i, z, 1 - c)))
-        if q == 0:
-            start(side_frames)
+            start(remote(("bank", q, d), part, block(q, i, c), at(tmpl_plus(2 * d), z, c)))
+        start(remote(("core", q), part, block(q, i, c), at(i, z, 1 - c)))
+
+    send_bank(0)
+    send_bank(1)
+    start(side_frames)
 
     def arrive(q):
         if q >= chunks:
             return
+        send_bank(q + 2)
         for d in range(1, half):
-            there = half_block(q, tmpl_plus(-2 * d), c, mine_half)
-            remote(("bank", q, d), there, there, at(i, near, c)).wait_recv()
-            start(remote(("near", q, d), there, there, at(i, near, c)))
-            start(remote(("pass", q, d, 0), there, there, at(i, z, 1 - c)))
-
-    def arrive_near(q):
-        if q >= chunks:
-            return
-        for d in range(1, half):
-            there = half_block(q, tmpl_plus(-2 * d), c, 1 - mine_half)
-            remote(("near", q, d), there, there, at(i, near, c)).wait_recv()
-            start(remote(("pass", q, d, 1), there, there, at(i, z, 1 - c)))
+            there = block(q, tmpl_plus(-2 * d), c)
+            remote(("bank", q, d), there, there, at(i, z, 1 - c)).wait_recv()
+            start(remote(("pass", q, d), there, there, at(i, z, 1 - c)))
 
     def finish(q):
         own_bank[q].wait()
         here = block(q, i, 1 - c)
         remote(("core", q), here, here, at(i, z, 1 - c)).wait_recv()
         for d in range(1, half):
-            for k, which in ((0, mine_half), (1, 1 - mine_half)):
-                there = half_block(q, tmpl_plus(-2 * d), 1 - c, which)
-                remote(("pass", q, d, k), there, there, at(i, z, 1 - c)).wait_recv()
+            there = block(q, tmpl_plus(-2 * d), 1 - c)
+            remote(("pass", q, d), there, there, at(i, z, 1 - c)).wait_recv()
 
     def unfold(g):
         @pl.when(z < n_tm - 1)
@@ -188,30 +178,20 @@
         labels[g, 0:id_rows, :] = jnp.broadcast_to(first, (id_rows, 128))
         labels[g, id_rows:2 * id_rows, :] = jnp.broadcast_to(second, (id_rows, 128))
 
-    def correlate(q):
+    def correlate(g, q):
         first = q * HALF // SHIFTS * SHIFTS
         lanes = slice(q * depth % unfolded.shape[2], q * depth % unfolded.shape[2] + depth)
-        part = lax.dot_general(
-            unfolded[0, first:first + length, lanes], weights[q],
-            (((1,), (1,)), ((), ())), preferred_element_type=jnp.float32)
-        if q == 0:
-            scores[0] = part
-        else:
-            scores[0] += part
-
-    def correlate_all(g):
+
         @pl.loop(0, length // ROWS)
         def _(step):
             base = pl.multiple_of(step * ROWS, ROWS)
-            total = None
-            for q in range(chunks):
-                first = q * HALF // SHIFTS * SHIFTS
-                lanes = slice(q * depth % unfolded.shape[2], q * depth % unfolded.shape[2] + depth)
-                part = lax.dot_general(
-                    unfolded[g, pl.ds(pl.multiple_of(base + first, SHIFTS), ROWS), lanes], weights[q],
-                    (((1,), (1,)), ((), ())), preferred_element_type=jnp.float32)
-                total = part if total is None else total + part
-            scores[g, pl.ds(base, ROWS), :] = total
+            part = lax.dot_general(
+                unfolded[g, pl.ds(pl.multiple_of(base + first, SHIFTS), ROWS), lanes], weights[q],
+                (((1,), (1,)), ((), ())), preferred_element_type=jnp.float32)
+            if q == 0:
+                scores[g, pl.ds(base, ROWS), :] = part
+            else:
+                scores[g, pl.ds(base, ROWS), :] += part
 
     def log_of(peak, total):
         return jnp.where(total > 0.0, peak + jnp.log(total), LOW)
@@ -242,24 +222,31 @@
     own_meta.wait()
     unfold(0)
     arrive(0)
-    arrive(1)
-    arrive_near(0)
-    arrive(2)
-    arrive_near(1)
     finish(0)
-    for q in range(chunks):
-        correlate(q)
-        arrive(q + 3)
-        arrive_near(q + 2)
-        if q + 1 < chunks:
+    early = chunks // 2
+    for q in range(early):
+        correlate(0, q)
+        arrive(q + 1)
+        if q + 1 < early:
             finish(q + 1)
-    summarize(0)
-    for dz in range(1, n_tm):
-        start(remote(("own", dz), stats.at[0], slabs.at[z, parity], at(i, tm_plus(dz), c)))
     side_frames.wait_recv()
     side_meta.wait_recv()
     unfold(1)
-    correlate_all(1)
+    for q in range(early):
+        correlate(1, q)
+        if q == 1:
+            arrive(early + 1)
+    finish(early)
+    for q in range(early, chunks):
+        correlate(0, q)
+        arrive(q + 2)
+        if q + 1 == chunks:
+            summarize(0)
+            for dz in range(1, n_tm):
+                start(remote(("own", dz), stats.at[0], slabs.at[z, parity], at(i, tm_plus(dz), c)))
+        correlate(1, q)
+        if q + 1 < chunks:
+            finish(q + 1)
     summarize(1)
     for dz in range(n_tm):
         start(remote(("side", dz), stats.at[1], slabs.at[z, parity], at(side, tm_plus(dz), c)))
@@ -322,7 +309,7 @@
     cols = rows * n
     meta = jnp.concatenate(
         [rec_ids.reshape(id_rows, 128), jnp.broadcast_to(valid_frames.reshape(1, 1), (8, 128))], axis=0)
-    copies = 6 + chunks * 2 * n + 2 * n_tm + 2 * n
+    copies = 6 + chunks * n + 2 * n_tm + 2 * n
     f32, bf16, i32 = jnp.float32, jnp.bfloat16, jnp.int32
     rec_half, top_half = pl.pallas_call(
         functools.partial(kernel, n, n_tm, (span * bins) ** (-0.5)),

time: 65 us -> 58.1 us (0.89)
  Pallas kernels: 60.2 us -> 53.2 us
    pallas_call x1, Pallas kernels: 60.2 us -> 53.2 us  [on_device(): pl.pallas_call(functools.partial(kernel, n, n_tm, (span * bins) ** (-0.5)...]
where the time goes in v3:
time: 58.1 us; the launch traced here: 57.9 us
  Pallas kernels  53.2 us (92%)
  local copies, waits for them, and re-layouts  3.28 us (6%)
  between operations  1.33 us (2%)
    pallas_call x1, Pallas kernels, on_device(): pl.pallas_call(functools.partial(kernel, n, n_tm, (span * bins) ** (-0.5)...  53.2 us
    unnamed x6, local copies, waits for them, and re-layouts  2.59 us

profile of v3, /device:TPU:0, one launch (start us, length us, event | category | flops | bytes accessed | tf_op | source)
XLA Modules:
  0.0 57.9 jit_solution(7475605605698891690)
XLA Ops:
  0.6 0.0 copy-start.1
  1.3 0.0 copy-done.1
  1.3 0.0 copy-start
  1.3 2.0 %copy.11 = bf16[8,8,64,128]{3,1,2,0:T(8,128)(2,1)S(1)} copy(bf16[8,8,64,128]{3,2,1,0:T(8,128)(2,1)} %bitcast.17) | data formatting | bytes 2097152
  3.3 0.0 copy-done
  3.3 53.2 %shard_map.59 = (f32[2,16,256]{2,1,0:T(8,128)S(1)}, f32[2,256]{1,0:T(2,128)S(1)}) custom-call(bf16[2048,128]{1,0:T(8,128)(2,1)S(1)} %bitcast.15, bf16[64,8192]{1,0:T(8,128)(2,1)S(1)} %bitcast.14, s32[24,128]{1,0:T(8,128)S(1)} %concatenate.3.meta), custom_call_target="tpu_custom_call" | custom-call | tf_op jit(solution)/shard_map/pallas_call | solution.py:314
  56.6 0.6 %reshape.25 = f32[1,16,512]{2,1,0:T(8,128)} reshape(f32[16,2,2,128]{3,2,1,0:T(2,128)S(1)} %copy.7) | data formatting | bytes 65536 | tf_op jit(solution)/shard_map/reshape | solution.py:342
  57.3 0.6 copy.14
  (3 shorter events, 0.0 us)
Async XLA Ops:
  0.6 0.7 %copy-start.1 = (s32[1,2048]{1,0:T(1,128)S(1)}, s32[1,2048]{1,0:T(1,128)}, u32[]{:S(2)}) copy-start(s32[1,2048]{1,0:T(1,128)} %param.6) | copy-start | bytes 24580
  1.3 2.0 %copy-start = (bf16[1,2048,128]{2,1,0:T(8,128)(2,1)S(1)}, bf16[1,2048,128]{2,1,0:T(8,128)(2,1)}, u32[]{:S(2)}) copy-start(bf16[1,2048,128]{2,1,0:T(8,128)(2,1)} %param.4) | copy-start | bytes 1572868

commit v4 on v1

--- a/solution.py
+++ b/solution.py
@@ -9,7 +9,7 @@
 
 RECS = 16
 SHIFTS = 16
-ROWS = 512
+ROWS = 1024
 PIECE = 64
 LOW = -1e30
 MESH = pl.DeviceIdType.MESH
@@ -59,6 +59,14 @@
         shard = (j // 2) * 2 + cc
         return weights.at[q, pl.ds(pl.multiple_of(shard * rows, 16), rows)]
 
+    barrier = pltpu.get_barrier_semaphore()
+    partners = [at(tmpl_plus(dj), z, c if dc == 0 else 1 - c)
+                for dj in range(n) for dc in range(2) if dj or dc]
+    for dz in range(1, n_tm):
+        partners += [at(i, tm_plus(dz), c), at(side, tm_plus(dz), c)]
+    for device in partners:
+        pl.semaphore_signal(barrier, inc=1, device_id=device, device_id_type=MESH)
+
     own_frames = pltpu.make_async_copy(corpus, frames.at[0, pl.ds(0, length)], local_sem.at[0])
     own_meta = pltpu.make_async_copy(meta, ids.at[0], local_sem.at[1])
     own_frames.start()
@@ -69,13 +77,6 @@
             bank.at[:, pl.ds(q * depth, depth)], block(q, i, c), local_sem.at[2 + q]))
         own_bank[-1].start()
 
-    barrier = pltpu.get_barrier_semaphore()
-    partners = [at(tmpl_plus(dj), z, c if dc == 0 else 1 - c)
-                for dj in range(n) for dc in range(2) if dj or dc]
-    for dz in range(1, n_tm):
-        partners += [at(i, tm_plus(dz), c), at(side, tm_plus(dz), c)]
-    for device in partners:
-        pl.semaphore_signal(barrier, inc=1, device_id=device, device_id_type=MESH)
     pl.semaphore_wait(barrier, len(partners))
 
     sent = []
@@ -181,8 +182,11 @@
             else:
                 scores[g, pl.ds(base, ROWS), :] += part
 
+    def log_of(peak, total):
+        return jnp.where(total > 0.0, peak + jnp.log(total), LOW)
+
     def summarize(g):
-        @pl.loop(0, id_rows)
+        @pl.loop(0, id_rows, unroll=2)
         def _(r):
             for h in range(2):
                 base = pl.multiple_of(r * 128 + h * PIECE, PIECE)
@@ -201,8 +205,7 @@
             mine = name == r
             peak = jnp.max(jnp.where(mine, tops, 0.0), axis=0, keepdims=True)
             total = jnp.sum(jnp.where(mine, sums * jnp.exp(jnp.minimum(tops - peak, 0.0)), 0.0), axis=0, keepdims=True)
-            stats[g, r:r + 1, :] = peak
-            stats[g, RECS + r:RECS + r + 1, :] = total
+            stats[g, r:r + 1, :] = log_of(peak, total)
 
     own_frames.wait()
     own_meta.wait()
@@ -235,17 +238,16 @@
         remote(("own", dz), there, there, at(i, tm_plus(-dz), c)).wait_recv()
 
     for h in range(2):
-        peak = slabs[0, h, 0:RECS, :]
+        peak = jnp.maximum(slabs[0, h], 0.0)
         for s in range(1, n_tm):
-            peak = jnp.maximum(peak, slabs[s, h, 0:RECS, :])
+            peak = jnp.maximum(peak, slabs[s, h])
         total = jnp.zeros_like(peak)
         for s in range(n_tm):
-            total += slabs[s, h, RECS:2 * RECS, :] * jnp.exp(slabs[s, h, 0:RECS, :] - peak)
+            total += jnp.exp(slabs[s, h] - peak)
         rec_out[h] = peak + jnp.log(jnp.exp(-peak) + total)
         top = jnp.max(peak, axis=0, keepdims=True)
-        group[2 * h:2 * h + 1, :] = top
-        group[2 * h + 1:2 * h + 2, :] = jnp.sum(total * jnp.exp(peak - top), axis=0, keepdims=True)
-    group[4:8, :] = jnp.zeros((4, cols), jnp.float32)
+        group[h:h + 1, :] = log_of(top, jnp.sum(total * jnp.exp(peak - top), axis=0, keepdims=True))
+    group[2:8, :] = jnp.zeros((6, cols), jnp.float32)
 
     mine = 2 * i + c
     for dj in range(n):
@@ -259,14 +261,13 @@
             if dj or dc:
                 there = groups_all.at[2 * tmpl_plus(-dj) + (c if dc == 0 else 1 - c)]
                 remote(("group", dj, dc), there, there, at(tmpl_plus(-dj), z, c if dc == 0 else 1 - c)).wait_recv()
-    for h in range(2):
-        top = groups_all[0, 2 * h:2 * h + 1, :]
-        for s in range(1, 2 * n):
-            top = jnp.maximum(top, groups_all[s, 2 * h:2 * h + 1, :])
-        total = jnp.zeros_like(top)
-        for s in range(2 * n):
-            total += groups_all[s, 2 * h + 1:2 * h + 2, :] * jnp.exp(groups_all[s, 2 * h:2 * h + 1, :] - top)
-        top_out[h:h + 1, :] = top + jnp.log(jnp.exp(-top) + total)
+    top = jnp.maximum(groups_all[0, 0:2, :], 0.0)
+    for s in range(1, 2 * n):
+        top = jnp.maximum(top, groups_all[s, 0:2, :])
+    total = jnp.zeros_like(top)
+    for s in range(2 * n):
+        total += jnp.exp(groups_all[s, 0:2, :] - top)
+    top_out[...] = top + jnp.log(jnp.exp(-top) + total)
 
     for copy in sent:
         copy.wait_send()
@@ -306,8 +307,8 @@
             pltpu.VMEM((2, 2 * id_rows, 128), i32),
             pltpu.VMEM((cols // 128, 2 * id_rows, 128), f32),
             pltpu.VMEM((cols // 128, 2 * id_rows, 128), f32),
-            pltpu.VMEM((2, 2 * RECS, cols), f32),
-            pltpu.VMEM((n_tm, 2, 2 * RECS, cols), f32),
+            pltpu.VMEM((2, RECS, cols), f32),
+            pltpu.VMEM((n_tm, 2, RECS, cols), f32),
             pltpu.VMEM((8, cols), f32),
             pltpu.VMEM((2 * n, 8, cols), f32),
             pltpu.SemaphoreType.DMA((2 + chunks,)),

time: 57.9 us -> 54.1 us (0.934)
  Pallas kernels: 53 us -> 49.3 us
    pallas_call x1, Pallas kernels: 53 us -> 49.3 us  [on_device(): pl.pallas_call(functools.partial(kernel, n, n_tm, (span * bins) ** (-0.5)...]
where the time goes in v4:
time: 54.1 us; the launch traced here: 53.9 us
  Pallas kernels  49.3 us (91%)
  local copies, waits for them, and re-layouts  3.28 us (6%)
  between operations  1.33 us (2%)
    pallas_call x1, Pallas kernels, on_device(): pl.pallas_call(functools.partial(kernel, n, n_tm, (span * bins) ** (-0.5)...  49.3 us
    unnamed x6, local copies, waits for them, and re-layouts  2.59 us

profile of v4, /device:TPU:0, one launch (start us, length us, event | category | flops | bytes accessed | tf_op | source)
XLA Modules:
  0.0 53.9 jit_solution(8061562814909870458)
XLA Ops:
  0.6 0.0 copy-start.1
  1.3 0.0 copy-done.1
  1.3 0.0 copy-start
  1.3 2.0 %copy.11 = bf16[8,8,64,128]{3,1,2,0:T(8,128)(2,1)S(1)} copy(bf16[8,8,64,128]{3,2,1,0:T(8,128)(2,1)} %bitcast.17) | data formatting | bytes 2097152
  3.3 0.0 copy-done
  3.3 49.3 %shard_map.59 = (f32[2,16,256]{2,1,0:T(8,128)S(1)}, f32[2,256]{1,0:T(2,128)S(1)}) custom-call(bf16[2048,128]{1,0:T(8,128)(2,1)S(1)} %bitcast.15, bf16[64,8192]{1,0:T(8,128)(2,1)S(1)} %bitcast.14, s32[24,128]{1,0:T(8,128)S(1)} %concatenate.3.meta), custom_call_target="tpu_custom_call" | custom-call | tf_op jit(solution)/shard_map/pallas_call | solution.py:293
  52.7 0.6 %reshape.25 = f32[1,16,512]{2,1,0:T(8,128)} reshape(f32[16,2,2,128]{3,2,1,0:T(2,128)S(1)} %copy.7) | data formatting | bytes 65536 | tf_op jit(solution)/shard_map/reshape | solution.py:321
  53.3 0.6 %copy.14 = f32[512]{0:T(512)} copy(f32[512]{0:T(512)S(1)} %bitcast.16) | data formatting | bytes 4096
  (3 shorter events, 0.0 us)
Async XLA Ops:
  0.6 0.7 %copy-start.1 = (s32[1,2048]{1,0:T(1,128)S(1)}, s32[1,2048]{1,0:T(1,128)}, u32[]{:S(2)}) copy-start(s32[1,2048]{1,0:T(1,128)} %param.6) | copy-start | bytes 24580
  1.3 2.0 %copy-start = (bf16[1,2048,128]{2,1,0:T(8,128)(2,1)S(1)}, bf16[1,2048,128]{2,1,0:T(8,128)(2,1)}, u32[]{:S(2)}) copy-start(bf16[1,2048,128]{2,1,0:T(8,128)(2,1)} %param.4) | copy-start | bytes 1572868

commit v5 on v4

--- a/solution.py
+++ b/solution.py
@@ -186,7 +186,7 @@
         return jnp.where(total > 0.0, peak + jnp.log(total), LOW)
 
     def summarize(g):
-        @pl.loop(0, id_rows, unroll=2)
+        @pl.loop(0, id_rows, unroll=4)
         def _(r):
             for h in range(2):
                 base = pl.multiple_of(r * 128 + h * PIECE, PIECE)

time: 54.1 us -> 53.9 us (level)
  no operation moved by 1% of the time
where the time goes in v5:
time: 53.9 us; the launch traced here: 53.7 us
  Pallas kernels  49.1 us (91%)
  local copies, waits for them, and re-layouts  3.28 us (6%)
  between operations  1.33 us (2%)
    pallas_call x1, Pallas kernels, on_device(): pl.pallas_call(functools.partial(kernel, n, n_tm, (span * bins) ** (-0.5)...  49.1 us
    unnamed x6, local copies, waits for them, and re-layouts  2.59 us

profile of v5, /device:TPU:0, one launch (start us, length us, event | category | flops | bytes accessed | tf_op | source)
XLA Modules:
  0.0 53.7 jit_solution(13153946745794634285)
XLA Ops:
  0.6 0.0 copy-start.1
  1.3 0.0 copy-done.1
  1.3 0.0 copy-start
  1.3 2.0 %copy.11 = bf16[8,8,64,128]{3,1,2,0:T(8,128)(2,1)S(1)} copy(bf16[8,8,64,128]{3,2,1,0:T(8,128)(2,1)} %bitcast.17) | data formatting | bytes 2097152
  3.3 0.0 copy-done
  3.3 49.1 %shard_map.59 = (f32[2,16,256]{2,1,0:T(8,128)S(1)}, f32[2,256]{1,0:T(2,128)S(1)}) custom-call(bf16[2048,128]{1,0:T(8,128)(2,1)S(1)} %bitcast.15, bf16[64,8192]{1,0:T(8,128)(2,1)S(1)} %bitcast.14, s32[24,128]{1,0:T(8,128)S(1)} %concatenate.3.meta), custom_call_target="tpu_custom_call" | custom-call | tf_op jit(solution)/shard_map/pallas_call | solution.py:293
  52.5 0.6 %reshape.25 = f32[1,16,512]{2,1,0:T(8,128)} reshape(f32[16,2,2,128]{3,2,1,0:T(2,128)S(1)} %copy.7) | data formatting | bytes 65536 | tf_op jit(solution)/shard_map/reshape | solution.py:321
  53.1 0.6 %copy.14 = f32[512]{0:T(512)} copy(f32[512]{0:T(512)S(1)} %bitcast.16) | data formatting | bytes 4096
  (3 shorter events, 0.0 us)
Async XLA Ops:
  0.6 0.7 %copy-start.1 = (s32[1,2048]{1,0:T(1,128)S(1)}, s32[1,2048]{1,0:T(1,128)}, u32[]{:S(2)}) copy-start(s32[1,2048]{1,0:T(1,128)} %param.6) | copy-start | bytes 24580
  1.3 2.0 %copy-start = (bf16[1,2048,128]{2,1,0:T(8,128)(2,1)S(1)}, bf16[1,2048,128]{2,1,0:T(8,128)(2,1)}, u32[]{:S(2)}) copy-start(bf16[1,2048,128]{2,1,0:T(8,128)(2,1)} %param.4) | copy-start | bytes 1572868
